TPU v7x, 512 devices: a whole 4x8x8 slice. The times are simulated.
512 devices in a mesh: tile: 128 (over y, z, core), dp: 4 (over x).
Axes of the slice: x: 4, y: 8, z: 8, core: 2. Of those that a mesh axis runs over, the one named last changes fastest.
Arguments:
- features: bfloat16 [4, 1024, 128, 128], P('dp', 'tile'), may hold values from -6 to 6
- w_sub: bfloat16 [27, 128, 128], replicated, may hold values from -0.109375 to 0.109375
- w_down: bfloat16 [8, 128, 256], replicated, may hold values from -0.1875 to 0.1875
- cotangent: bfloat16 [4, 512, 128, 256], P('dp', 'tile'), may hold values from -6 to 6
- vox_mask: int32 [4, 1024, 128], P('dp', 'tile'), may hold values from 0 to 1, as said below
- nbr_owner: int32 [4, 1024, 27], P('dp', 'tile'), may hold values from -1 to 127, as said below
- nbr_slot: int32 [4, 1024, 27], P('dp', 'tile'), may hold values from 0 to 7, as said below
- voxel_map: int32 [4, 1024, 27, 128], P('dp', 'tile'), may hold values from -1 to 127, as said below
- parent_slot: int32 [4, 1024], P('dp', 'tile'), may hold values from 0 to 3, as said below
- parent_octant: int32 [4, 1024], P('dp', 'tile'), may hold values from 0 to 7, as said below
Outputs:
- coarse_out: bfloat16 [4, 512, 128, 256], P('dp', 'tile')
- grad_input: bfloat16 [4, 1024, 128, 128], P('dp', 'tile')
- grad_sub_flat: float32 [442368], P('tile')
- grad_down_flat: float32 [262144], P('tile')
Inputs may be any that keep to these rules, and one draw needn't show every extreme that they name: `vox_mask`: in each tile the slots that hold only zeros lie just before its last 2 slots. `nbr_owner`: A neighbour lies on the block's own tile, on the tile before it (then in one of that tile's last 2 slots, and only for the first 2 blocks of a tile) or on the tile after it (then in one of its first 2 slots, and only for the last 2 blocks of a tile). Offset 13 is the block itself. `nbr_slot`: 0 where there is no neighbour. `voxel_map`: at offset 13 every voxel reads itself. `parent_slot`: each coarse block of a tile receives exactly two fine blocks of that tile. `parent_octant`: the two fine blocks of one coarse block have different octants.
All inputs are finite; a program needn't handle non-finite values.
Results may differ from a plain program's by a relative error of at most 0.007.
Values may be sent and summed in bfloat16 or wider, within the bound.
A program may use at most 64 MiB of HBM per device.

v0:
```python
import jax
import jax.numpy as jnp
from jax import lax
from jax.sharding import PartitionSpec as P

FACE = 2


def with_halo(x, sides, width):
    for axis, dim in sides:
        size, length = (lax.axis_size(axis), x.shape[dim])
        up = [(i, (i + 1) % size) for i in range(size - 1)]
        down = [(j, i) for i, j in up]
        last = lax.slice_in_dim(x, length - width, length, axis=dim)
        first = lax.slice_in_dim(x, 0, width, axis=dim)
        before = lax.ppermute(last, axis, up)
        after = lax.ppermute(first, axis, down)
        x = jnp.concatenate([before, x, after], axis=dim)
    return x


def to_children(fine_blocks):
    count, voxels, channels = fine_blocks.shape
    half_depth = voxels // 32
    shaped = fine_blocks.reshape(count, half_depth, 2, 2, 2, 2, 2, channels)
    shaped = jnp.transpose(shaped, (0, 2, 4, 6, 1, 3, 5, 7))
    return shaped.reshape(count, 8, voxels // 8, channels)


def from_children(child_blocks):
    count, eight, places, channels = child_blocks.shape
    half_depth = places // 4
    shaped = child_blocks.reshape(count, 2, 2, 2, half_depth, 2, 2, channels)
    shaped = jnp.transpose(shaped, (0, 4, 1, 5, 2, 6, 3, 7))
    return shaped.reshape(count, places * 8, channels)


def octants_to_block(octant_blocks):
    count, eight, places, channels = octant_blocks.shape
    half_depth = places // 4
    shaped = octant_blocks.reshape(count, 2, 2, 2, half_depth, 2, 2, channels)
    shaped = jnp.transpose(shaped, (0, 1, 4, 2, 5, 3, 6, 7))
    return shaped.reshape(count, places * 8, channels)


def block_to_octants(coarse_blocks):
    count, voxels, channels = coarse_blocks.shape
    half_depth = voxels // 32
    shaped = coarse_blocks.reshape(count, 2, half_depth, 2, 2, 2, 2, channels)
    shaped = jnp.transpose(shaped, (0, 1, 3, 5, 2, 4, 6, 7))
    return shaped.reshape(count, 8, voxels // 8, channels)


def return_terms(voxel_pick, block_pick, grads_bf, weights_f):
    spread = jnp.einsum("bkvu,bvd->bkud", voxel_pick, grads_bf, preferred_element_type=jnp.float32)
    terms = jnp.einsum("bkud,kcd->bkuc", spread, weights_f, precision=lax.Precision.HIGHEST)
    return jnp.einsum(
        "bke,bkuc->euc", block_pick.astype(jnp.float32), terms, precision=lax.Precision.HIGHEST
    )


def on_device(
    features,
    w_sub,
    w_down,
    cotangent,
    vox_mask,
    nbr_owner,
    nbr_slot,
    voxel_map,
    parent_slot,
    parent_octant,
):
    blocks = features.shape[1]
    voxels = features.shape[2]
    channels = features.shape[3]
    coarse_count = cotangent.shape[1]
    tile_index = lax.axis_index("tile")
    active = vox_mask[0] > 0
    keep_f = active.reshape(-1, 1).astype(jnp.float32)
    masked = jnp.where(active[:, :, None], features[0], jnp.zeros((), jnp.bfloat16))
    halo_width = FACE
    extended = with_halo(masked, (("tile", 0),), halo_width)
    ext_count = extended.shape[0]
    owner_tile = nbr_owner[0]
    slot_index = nbr_slot[0]
    position = jnp.where(
        owner_tile == tile_index - 1,
        slot_index - (blocks - halo_width),
        jnp.where(
            owner_tile == tile_index, halo_width + slot_index, halo_width + blocks + slot_index
        ),
    )
    block_pick = (
        (position[:, :, None] == jnp.arange(ext_count, dtype=jnp.int32)[None, None, :])
        & (owner_tile >= 0)[:, :, None]
    ).astype(jnp.bfloat16)
    voxel_pick = (
        voxel_map[0][:, :, :, None] == jnp.arange(voxels, dtype=jnp.int32)[None, None, None, :]
    ).astype(jnp.bfloat16)
    source_blocks = jnp.einsum(
        "bke,euc->bkuc", block_pick, extended, preferred_element_type=jnp.float32
    ).astype(jnp.bfloat16)
    gathered = jnp.einsum(
        "bkvu,bkuc->bkvc", voxel_pick, source_blocks, preferred_element_type=jnp.float32
    ).astype(jnp.bfloat16)
    pre_act = jnp.einsum(
        "bkvc,kcd->bvd", gathered, w_sub, preferred_element_type=jnp.float32
    ).reshape(-1, channels)
    hidden = (keep_f * jax.nn.silu(pre_act)).astype(jnp.bfloat16)
    children = to_children(hidden.reshape(blocks, voxels, channels))
    parent_pick = (
        parent_slot[0][:, None, None] == jnp.arange(coarse_count, dtype=jnp.int32)[None, :, None]
    ) & (parent_octant[0][:, None, None] == jnp.arange(8, dtype=jnp.int32)[None, None, :])
    partial_value = jnp.einsum(
        "ncuk,ckj->nuj", children, w_down, preferred_element_type=jnp.float32
    )
    coarse_oct = jnp.einsum(
        "nqo,nuj->qouj",
        parent_pick.astype(jnp.float32),
        partial_value,
        precision=lax.Precision.HIGHEST,
    )
    coarse_out = octants_to_block(coarse_oct).astype(jnp.bfloat16)[None]
    cot_oct = block_to_octants(cotangent[0])
    picked = jnp.einsum(
        "nqo,qouj->nuj",
        parent_pick.astype(jnp.bfloat16),
        cot_oct,
        preferred_element_type=jnp.float32,
    ).astype(jnp.bfloat16)
    dchildren = jnp.einsum("nuj,ckj->ncuk", picked, w_down, preferred_element_type=jnp.float32)
    grad_down = jnp.einsum("ncuk,nuj->ckj", children, picked, preferred_element_type=jnp.float32)
    dhidden = from_children(dchildren).reshape(-1, channels)
    sigmoid_pre = jax.nn.sigmoid(pre_act)
    dpre = (keep_f * dhidden * sigmoid_pre * (1.0 + pre_act * (1.0 - sigmoid_pre))).astype(
        jnp.bfloat16
    )
    dpre_blocks = dpre.reshape(blocks, voxels, channels)
    grad_sub = jnp.einsum(
        "bkvc,bvd->kcd", gathered, dpre_blocks, preferred_element_type=jnp.float32
    )
    weights_f = w_sub.astype(jnp.float32)
    grad_rows = return_terms(voxel_pick, block_pick, dpre_blocks, weights_f)
    own_grad = grad_rows[halo_width : halo_width + blocks]
    outgoing = jnp.concatenate([grad_rows[:halo_width], grad_rows[halo_width + blocks :]], axis=0)
    returned = with_halo(outgoing.astype(jnp.bfloat16), (("tile", 0),), halo_width).astype(
        outgoing.dtype
    )
    own_grad = own_grad.at[:halo_width].add(returned[:halo_width])
    own_grad = own_grad.at[blocks - halo_width :].add(returned[3 * halo_width :])
    grad_input = (keep_f.reshape(blocks, voxels, 1) * own_grad).astype(jnp.bfloat16)[None]
    grad_scale = float(lax.axis_size("dp") * lax.axis_size("tile") * blocks * voxels) ** (-0.5)
    flat_sub = grad_sub.reshape(-1)
    flat_down = grad_down.reshape(-1)
    total_sub, total_down = lax.psum((flat_sub, flat_down), ("tile", "dp"))
    width_sub = total_sub.shape[0] // lax.axis_size("tile")
    width_down = total_down.shape[0] // lax.axis_size("tile")
    share_sub = lax.dynamic_slice_in_dim(total_sub, tile_index * width_sub, width_sub, 0)
    share_down = lax.dynamic_slice_in_dim(total_down, tile_index * width_down, width_down, 0)
    return (coarse_out, grad_input, share_sub * grad_scale, share_down * grad_scale)


def solution(mesh):
    in_specs = (
        P("dp", "tile", None, None),
        P(),
        P(),
        P("dp", "tile", None, None),
        P("dp", "tile", None),
        P("dp", "tile", None),
        P("dp", "tile", None),
        P("dp", "tile", None, None),
        P("dp", "tile"),
        P("dp", "tile"),
    )
    out_specs = (P("dp", "tile", None, None), P("dp", "tile", None, None), P("tile"), P("tile"))
    return jax.shard_map(
        on_device, mesh=mesh, in_specs=in_specs, out_specs=out_specs, check_vma=False
    )
```

profile of v0, /device:TPU:1, one launch (start us, length us, event | category | flops | bytes accessed | tf_op | source)
XLA Modules:
  0.0 376.6 jit_solution(3792756882280352824)
XLA Ops:
  7.2 0.9 copy.62
  8.1 1.2 bitcast_select_fusion
  9.4 5.4 %collective-permute-start = (bf16[2,128,128]{2,0,1:T(2,128)(2,1)S(1)}, bf16[2,128,128]{2,0,1:T(2,128)(2,1)S(1)}, u32[]{:S(2)}, u32[]{:S(2)}) collective-permute-start(bf16[2,128,128]{2,0,1:T(2,128)(2,1)S(1)} %get-tuple-element.36), channel_id=1, source_target_pairs={{0,4},{4,8},{8,12},{12,16},{16,20},{20,24},{24,28},{28,32},{32,36}... | collective-permute-start | bytes 196616 | tf_op jit(solution)/shard_map/ppermute | solution.py:16
  14.8 4.7 %collective-permute-start.1 = (bf16[2,128,128]{2,0,1:T(2,128)(2,1)S(1)}, bf16[2,128,128]{2,0,1:T(2,128)(2,1)S(1)}, u32[]{:S(2)}, u32[]{:S(2)}) collective-permute-start(bf16[2,128,128]{2,0,1:T(2,128)(2,1)S(1)} %get-tuple-element.37), channel_id=1, source_target_pairs={{4,0},{8,4},{12,8},{16,12},{20,16},{24,20},{28,24},{32,28},{36,32}... | collective-permute-start | bytes 196616 | tf_op jit(solution)/shard_map/ppermute | solution.py:17
  20.1 0.7 iota_compare_fusion.3
  20.9 1.1 reshape_squeeze.3
  22.7 1.4 fusion.22
  25.5 0.9 copy.63
  26.7 4.6 %convolution_convert_fusion = bf16[8,27,128,128]{3,1,2,0:T(8,128)(2,1)} fusion(bf16[2,128,128]{2,0,1:T(2,128)(2,1)S(1)} %collective-permute-done.1, bf16[8,128,128]{2,0,1:T(8,128)(2,1)S(1)} %bitcast_select_fusion, bf16[2,128,128]{2,0,1:T(2,128)(2,1)S(1)} %collective-permute-done, s32[8,27]{1,0:T(8,128)S(1)} %select_bitcast_fusion, ...), kind=kOutput, calls=%fused_computation.8 | convolution fusion | flops 89658432 | bytes 7472184 | tf_op jit(solution)/shard_map/bke,euc->bkuc/dot_general | solution.py:101
  31.4 12.0 %fusion.6 = bf16[8,27,128,128]{3,2,1,0:T(8,128)(2,1)} fusion(bf16[8,27,128,128]{3,1,2,0:T(8,128)(2,1)} %convolution_convert_fusion, s32[8,27,128]{2,1,0:T(8,128)S(1)} %copy.63), kind=kOutput, calls=%fused_computation.9 | convolution fusion | flops 913047552 | bytes 14266368 | tf_op jit(solution)/shard_map/bkvu,bkuc->bkvc/dot_general | solution.py:104
  43.4 5.2 %multiply_convert_fusion.1 = (bf16[8,128,128]{2,1,0:T(8,128)(2,1)S(1)}, f32[8,128,128]{2,1,0:T(8,128)S(1)}) fusion(f32[8,128,128]{2,1,0:T(8,128)S(1)} %bitcast.118, f32[8,128]{1,0:T(8,128)S(1)} %copy.72, bf16[8,27,128,128]{3,2,1,0:T(8,128)(2,1)} %fusion.6, bf16[27,128,128]{2,1,0:T(8,128)(2,1)S(1)} %copy-done), kind=kOutput, calls=%fused_computation.28 | convolution fusion | flops 907280384 | bytes 9277440 | tf_op jit(solution)/shard_map/bkvc,kcd->bvd/dot_general | solution.py:107
  48.6 3.3 fusion.25
  51.9 2.0 fusion.2
  54.8 1.7 copy.106
  56.6 9.0 %convolution_bitcast_fusion = f32[8,27,128,128]{3,2,0,1:T(8,128)} fusion(f32[8,27,128,128]{3,2,0,1:T(8,128)S(1)} %fusion.2, bf16[27,128,128]{2,1,0:T(8,128)(2,1)S(1)} %copy-done), kind=kOutput, calls=%fused_computation.5 | convolution fusion | flops 5435817984 | bytes 29196288 | tf_op jit(solution)/shard_map/bkud,kcd->bkuc/dot_general | solution.py:56
  65.6 18.4 %fusion.9 = f32[12,128,128]{2,0,1:T(8,128)S(1)} fusion(f32[8,27,128,128]{3,2,0,1:T(8,128)} %convolution_bitcast_fusion, s32[8,27]{1,0:T(8,128)S(1)} %select_bitcast_fusion, pred[8,27]{1,0:T(8,128)(4,1)S(1)} %compare_bitcast_fusion), kind=kOutput, calls=%fused_computation.10 | convolution fusion | flops 509613120 | bytes 14943288 | tf_op jit(solution)/shard_map/bke,bkuc->euc/dot_general | solution.py:57
  84.4 1.9 collective-permute-start.2
  86.3 2.4 collective-permute-start.3
  89.8 0.8 convert_element_type.75
  90.7 1.2 collective-permute-done.3
  92.0 0.9 fusion.24
  92.9 274.2 %all-reduce.3.cloned.1.call-done = (f32[442368]{0:T(1024)}, f32[262144]{0:T(1024)}) async-done(((f32[442368]{0:T(1024)}, f32[262144]{0:T(1024)}), (f32[442368]{0:T(1024)}, f32[262144]{0:T(1024)})) %all-reduce.3.cloned.1.call-update) | async-done | bytes 2818064 | tf_op jit(solution)/shard_map/psum | solution.py:156
  367.0 1.4 dynamic-slice_multiply_fusion
  368.5 1.3 dynamic-slice_multiply_fusion.1
  (35 shorter events, 5.6 us)
Async XLA Ops:
  7.2 36.2 %copy-start = (bf16[27,128,128]{2,1,0:T(8,128)(2,1)S(1)}, bf16[27,128,128]{2,1,0:T(8,128)(2,1)}, u32[]{:S(2)}) copy-start(bf16[27,128,128]{2,1,0:T(8,128)(2,1)} %param.15) | copy-start | bytes 2654212
  7.2 359.9 %all-reduce.3.cloned.1.call-start = ((), (), s32[]{:S(2)}) async-start(), calls=%async_computation | async-start | bytes 5636096 | tf_op jit(solution)/shard_map/psum | solution.py:156
  9.4 17.4 %collective-permute-start = (bf16[2,128,128]{2,0,1:T(2,128)(2,1)S(1)}, bf16[2,128,128]{2,0,1:T(2,128)(2,1)S(1)}, u32[]{:S(2)}, u32[]{:S(2)}) collective-permute-start(bf16[2,128,128]{2,0,1:T(2,128)(2,1)S(1)} %get-tuple-element.36), channel_id=1, source_target_pairs={{0,4},{4,8},{8,12},{12,16},{16,20},{20,24},{24,28},{28,32},{32,36}... | collective-permute-start | bytes 196616 | tf_op jit(solution)/shard_map/ppermute | solution.py:16
  14.8 12.0 %collective-permute-start.1 = (bf16[2,128,128]{2,0,1:T(2,128)(2,1)S(1)}, bf16[2,128,128]{2,0,1:T(2,128)(2,1)S(1)}, u32[]{:S(2)}, u32[]{:S(2)}) collective-permute-start(bf16[2,128,128]{2,0,1:T(2,128)(2,1)S(1)} %get-tuple-element.37), channel_id=1, source_target_pairs={{4,0},{8,4},{12,8},{16,12},{20,16},{24,20},{28,24},{32,28},{36,32}... | collective-permute-start | bytes 196616 | tf_op jit(solution)/shard_map/ppermute | solution.py:17
  43.4 5.3 %copy-start.1 = (bf16[8,27,128,128]{3,2,1,0:T(8,128)(2,1)S(1)}, bf16[8,27,128,128]{3,2,1,0:T(8,128)(2,1)}, u32[]{:S(2)}) copy-start(bf16[8,27,128,128]{3,2,1,0:T(8,128)(2,1)} %fusion.6) | copy-start | bytes 21233668
  65.6 23.1 %copy-start.2 = (bf16[8,128,256]{2,1,0:T(8,128)(2,1)S(1)}, bf16[8,128,256]{2,1,0:T(8,128)(2,1)}, u32[]{:S(2)}) copy-start(bf16[8,128,256]{2,1,0:T(8,128)(2,1)} %param.16) | copy-start | bytes 1572868
  84.4 6.3 %collective-permute-start.2 = (bf16[2,128,128]{2,1,0:T(8,128)(2,1)S(1)}, bf16[2,128,128]{2,1,0:T(8,128)(2,1)S(1)}, u32[]{:S(2)}, u32[]{:S(2)}) collective-permute-start(bf16[2,128,128]{2,1,0:T(8,128)(2,1)S(1)} %get-tuple-element.34), channel_id=1, source_target_pairs={{0,4},{4,8},{8,12},{12,16},{16,20},{20,24},{24,28},{28,32},{32,36}... | collective-permute-start | bytes 196616 | tf_op jit(solution)/shard_map/ppermute | solution.py:16
  86.3 5.6 %collective-permute-start.3 = (bf16[2,128,128]{2,1,0:T(8,128)(2,1)S(1)}, bf16[2,128,128]{2,1,0:T(8,128)(2,1)S(1)}, u32[]{:S(2)}, u32[]{:S(2)}) collective-permute-start(bf16[2,128,128]{2,1,0:T(8,128)(2,1)S(1)} %get-tuple-element.35), channel_id=1, source_target_pairs={{4,0},{8,4},{12,8},{16,12},{20,16},{24,20},{28,24},{32,28},{36,32}... | collective-permute-start | bytes 196616 | tf_op jit(solution)/shard_map/ppermute | solution.py:17
Sparse Core Ops, SparseCore 0:
  84.5 282.5 all-reduce.2
where the time goes:
time: 378 us; the launch traced here: 377 us
  waiting for transfers between devices  275 us (73%)
  matrix products  57.4 us (15%)
  starting transfers between devices  14.4 us (4%)
  between operations  14.3 us (4%)
  other arithmetic  8.1 us (2%)
  local copies, waits for them, and re-layouts  6.91 us (2%)
    psum x1, waiting for transfers between devices, on_device(): total_sub, total_down = lax.psum((flat_sub, flat_down), ('tile', 'dp'))  274 us
    dot_general x1, matrix products, return_terms(): jnp.einsum('bke,bkuc->euc', block_pick.astype(jnp.float32), terms, precis...  18.4 us
    dot_general x1, matrix products, on_device(): jnp.einsum('bkvu,bkuc->bkvc', voxel_pick, source_blocks, preferred_elemen...  12 us
    dot_general x1, matrix products, return_terms(): jnp.einsum('bkud,kcd->bkuc', spread, weights_f, precision=lax.Precision.H...  9.04 us
  transfers between devices with their start and end apart: 5, of which 2 were waited for; matrix products, arithmetic and copies ran while one was open for 3% of the time, Pallas kernels for 0%

commit v1 on v0

v1 whole, which is shorter than its diff:
```python
import functools

import jax
import jax.numpy as jnp
from jax import lax
from jax.experimental import pallas as pl
from jax.experimental.pallas import tpu as pltpu
from jax.sharding import PartitionSpec as P

FACE = 2
MESH = pl.DeviceIdType.MESH
TILE_ROWS = 8
HALF_T = 3
PITCH = 32
NO_BLOCK = 99
NO_VOXEL = 1000


def child_order(shape):
    new = lax.broadcasted_iota(jnp.int32, shape, 1)
    child, place = new // 16, new % 16
    z = 2 * (place // 4) + child // 4
    y = 2 * ((place // 2) % 2) + (child // 2) % 2
    x = 2 * (place % 2) + child % 2
    return 16 * z + 4 * y + x


def dot(a, b, dims=((1,), (0,))):
    return lax.dot_general(a, b, (dims, ((), ())), preferred_element_type=jnp.float32)


def sort_rows(e_row, count):
    wide = e_row.shape[1]
    square = (wide, wide)
    down = lax.broadcasted_iota(jnp.int32, square, 0)
    along = lax.broadcasted_iota(jnp.int32, square, 1)
    theirs = jnp.broadcast_to(e_row, square)
    mine = theirs.T

    def total(where, value=1):
        return jnp.sum(jnp.where(where, value, 0), axis=0, keepdims=True)

    rank = total((mine < theirs) | ((mine == theirs) & (down < along)))
    rank_down = jnp.broadcast_to(rank, square).T
    order = jnp.minimum(total(rank_down == along, down), count - 1)
    same = jnp.where(
        total(rank_down == along, mine) == total(rank_down == along - 1, mine), 1, 0
    )
    last = jnp.clip(total(mine <= along) - 1, 0, count - 1)
    some = jnp.minimum(total(mine == along), 1)
    return order, order // TILE_ROWS, same, last, some


def kernel(
    sizes, scale, table_ref, erow_ref, feat_ref, map_ref, ws_ref, wd_ref, cot_ref,
    mask_ref, coarse_ref, grad_ref, sub_ref, down_ref,
    picks, gathered, ext_t, halo_in, ws_t, ws_k, spread_v, map_p, pre_t, hidden, factor, dpre, pairs,
    grad_sub, grad_down, sort_v, sort_s, seg, parts,
    send0, recv0, acc1, send1, recv1, acc2, recv2, recv3, share, out_h, in_h,
    sort_sem, ss0, rs0, ss1, rs1, ss2, rs2, ss3, rs3, ssh, rsh, ssg, rsg,
):
    f32, bf16 = jnp.float32, jnp.bfloat16
    nx, ny, nz = sizes
    tile = lax.axis_index("tile")
    x = lax.axis_index("dp")
    core = lax.rem(tile, 2)
    z = lax.rem(tile // 2, nz)
    y = tile // (2 * nz)
    other = 1 - core
    count = 2 * ny * nz

    def place(yy, zz, cc):
        return (yy * nz + zz) * 2 + cc

    x_peers = [lax.rem(x + d, nx) for d in range(1, nx)]
    y_peers = [lax.rem(y + d, ny) for d in range(1, ny)]
    z_peers = [lax.rem(z + d, nz) for d in range(1, nz)]
    after, before = lax.rem(tile + 1, count), lax.rem(tile + count - 1, count)

    barrier = pltpu.get_barrier_semaphore()
    peers = [(place(y, z, other), x), (after, x), (before, x)]
    peers += [(tile, xx) for xx in x_peers]
    peers += [(place(yy, z, core), x) for yy in y_peers]
    peers += [(place(y, zz, core), x) for zz in z_peers]
    for peer in peers:
        pl.semaphore_signal(barrier, inc=1, device_id=peer, device_id_type=MESH)

    copies = []

    def send(src, dst, ss, rs, t, xx):
        copy = pltpu.make_async_remote_copy(
            src_ref=src, dst_ref=dst, send_sem=ss, recv_sem=rs,
            device_id=(t, xx), device_id_type=MESH,
        )
        copy.start()
        copies.append(copy)
        return copy

    offsets, voxels, wide = picks.shape
    blocks = wide // voxels
    channels = ws_ref.shape[1]
    lanes = lambda b: pl.ds(b * voxels, voxels)

    masks = mask_ref[...].astype(bf16)
    for b in range(blocks):
        ext_t[FACE + b] = feat_ref[b].T * masks[b:b + 1]
    pl.semaphore_wait(barrier, len(peers))
    halo = [
        send(ext_t.at[pl.ds(FACE, FACE)], halo_in.at[1], ssh.at[0], rsh.at[0], before, x),
        send(ext_t.at[pl.ds(blocks, FACE)], halo_in.at[0], ssh.at[1], rsh.at[1], after, x),
    ]
    sort_v[...] = jnp.zeros_like(sort_v)
    for i, row in enumerate(sort_rows(erow_ref[...], offsets * blocks)):
        sort_v[i:i + 1, :] = row
    sort_copy = pltpu.make_async_copy(sort_v, sort_s, sort_sem)
    sort_copy.start()

    perm = (
        lax.broadcasted_iota(jnp.int32, (voxels, voxels), 0) == child_order((voxels, voxels))
    ).astype(bf16)
    for b in range(blocks):
        map_p[b, 0:offsets, :] = dot(map_ref[b].astype(bf16), perm)
    keep = dot(masks, perm)
    row_ids = lax.broadcasted_iota(jnp.int32, (voxels, voxels), 0).astype(f32)

    def transpose_weight(k, c):
        weight = ws_ref[k].T
        ws_k[k] = weight
        ws_t[:, pl.ds(pl.multiple_of(k * channels, channels), channels)] = weight
        return c

    def gather(some, weights):
        def body(k, c):
            if weights:
                transpose_weight(k, c)
            for b in some:
                row = map_p[b, pl.ds(k, 1), :] - table_ref[blocks + b, k].astype(f32)
                tile_bk = (row_ids == row).astype(bf16)
                picks[k, :, lanes(b)] = tile_bk
                gathered[k, :, lanes(b)] = dot(ext_t[table_ref[b, k]], tile_bk).astype(bf16)
            return c
        lax.fori_loop(0, offsets, body, 0, unroll=3)

    gather(range(FACE, blocks - FACE), True)
    for copy in halo:
        copy.wait_recv()
    for i in range(FACE):
        ext_t[i] = halo_in[0, i]
        ext_t[FACE + blocks + i] = halo_in[1, i]
    gather(list(range(FACE)) + list(range(blocks - FACE, blocks)), False)

    flat_g = gathered.reshape(offsets * channels, wide)
    flat_p = picks.reshape(offsets * voxels, wide)
    for p in range(blocks // 2):
        cols = pl.ds(p * 2 * voxels, 2 * voxels)
        pre_t[:, cols] = dot(ws_t[...], flat_g[:, cols])
    for b in range(blocks):
        pre = pre_t[:, lanes(b)]
        sig = jax.nn.sigmoid(pre)
        keep_b = keep[b:b + 1]
        hid = (keep_b * (pre * sig)).T.astype(bf16)
        for c in range(8):
            hidden[b * 16:(b + 1) * 16, c * channels:(c + 1) * channels] = hid[c * 16:(c + 1) * 16]
        factor[lanes(b), :] = (keep_b * sig * (1.0 + pre * (1.0 - sig))).T

    lane = lax.broadcasted_iota(jnp.int32, (1, voxels), 1)
    spot = lane % 16
    target = 16 * (spot // 4) + 4 * ((spot // 2) % 2) + spot % 2
    for b in range(blocks):
        target = target + jnp.where(lane // 16 == b, table_ref[2 * blocks, b], 0)
    scatter = (
        lax.broadcasted_iota(jnp.int32, (cot_ref.shape[0], voxels), 0) == target
    ).astype(bf16)
    partial_value = dot(hidden[...], wd_ref[...]).astype(bf16)
    coarse_ref[...] = dot(scatter, partial_value).astype(bf16)
    picked = dot(scatter, cot_ref[...], ((0,), (0,))).astype(bf16)
    dchildren = dot(picked, wd_ref[...], ((1,), (1,)))
    grad_down[...] = dot(hidden[...], picked, ((0,), (0,)))
    pairs[...] = jnp.zeros_like(pairs)
    for b in range(blocks):
        for c in range(8):
            rows = slice(b * voxels + c * 16, b * voxels + (c + 1) * 16)
            part = dchildren[b * 16:(b + 1) * 16, c * channels:(c + 1) * channels]
            dpre[rows, :] = (part * factor[rows, :]).astype(bf16)
        half = (b % 2) * voxels
        pairs[b // 2, half:half + voxels, half:half + voxels] = dpre[lanes(b), :]

    def weight_grad(j, c):
        rows = pl.ds(pl.multiple_of(j * 3 * channels, channels), 3 * channels)
        grad_sub[rows, :] = dot(flat_g[rows, :], dpre[...])
        return c

    lax.fori_loop(0, offsets // 3, weight_grad, 0)

    chip_rows = offsets * channels // (ny * nz)
    own = chip_rows // 2

    def stage(yy, c):
        first = pl.multiple_of(yy * nz * chip_rows, 16)
        slab = grad_sub[pl.ds(first, nz * chip_rows), :]
        down = grad_down[pl.ds(pl.multiple_of(yy * channels, channels), channels), :]
        for zz in range(nz):
            for cc in range(2):
                start = (zz * 2 + cc) * own
                parts[cc, 0, yy, zz] = slab[start:start + HALF_T * TILE_ROWS]
                rest = own - HALF_T * TILE_ROWS
                last = slab[start + HALF_T * TILE_ROWS:start + own]
                parts[cc, 1, zz, yy, 0:TILE_ROWS, :] = jnp.concatenate(
                    [last, jnp.zeros((TILE_ROWS - rest, channels), f32)], axis=0
                )
                start = (zz * 2 + cc) * TILE_ROWS
                for i in range(2):
                    rows = slice((i + 1) * TILE_ROWS, (i + 2) * TILE_ROWS)
                    parts[cc, 1, zz, yy, rows, :] = down[
                        start:start + TILE_ROWS, i * 128:(i + 1) * 128
                    ]
        return c

    lax.fori_loop(0, ny, stage, 0)

    step0 = []
    for h in range(2):
        def cast_half(i, c, h=h):
            send0[h, i] = parts[other, h, i].astype(bf16)
            return c
        lax.fori_loop(0, ny, cast_half, 0)
        step0.append(
            send(send0.at[h], recv0.at[h], ss0.at[h], rs0.at[h], place(y, z, other), x)
        )

    def spread(j, c):
        rows = pl.ds(pl.multiple_of(j * 3 * voxels, voxels), 3 * voxels)
        for p in range(blocks // 2):
            cols = pl.ds(p * 2 * voxels, 2 * voxels)
            both = dot(flat_p[rows, cols], pairs[p]).astype(bf16)
            for q in range(3):
                for i in range(2):
                    spread_v[(j * 3 + q) * blocks + 2 * p + i] = both[
                        q * voxels:(q + 1) * voxels, i * channels:(i + 1) * channels
                    ]
        return c

    lax.fori_loop(0, offsets // 3, spread, 0)

    step1 = []
    for h in range(2):
        step0[h].wait_recv()

        def add_core(i, c, h=h):
            total = parts[core, h, i] + recv0[h, i].astype(f32)
            acc1[h, i] = total
            send1[h, i] = total.astype(bf16)
            return c

        lax.fori_loop(0, ny, add_core, 0)
        for d in range(ny - 1):
            to = y_peers[d] if h == 0 else z_peers[d]
            t = place(to, z, core) if h == 0 else place(y, to, core)
            step1.append(send(send1.at[h, to], recv1.at[h, d], ss1.at[h, d], rs1.at[h, d], t, x))

    sort_copy.wait()

    def term(i, running):
        running = running * sort_s[2, i].astype(f32)
        running = running + dot(spread_v[sort_s[0, i]], ws_k[sort_s[1, i]])
        seg[i] = running
        return running

    lax.fori_loop(
        0, offsets * blocks, term, jnp.zeros((voxels, channels), f32), unroll=4
    )

    def block_grad(e):
        return seg[sort_s[3, e]] * sort_s[4, e].astype(f32)

    for i in range(FACE):
        out_h[0, i] = block_grad(i).astype(bf16)
        out_h[1, i] = block_grad(FACE + blocks + i).astype(bf16)
    returns = [
        send(out_h.at[0], in_h.at[1], ssg.at[0], rsg.at[0], before, x),
        send(out_h.at[1], in_h.at[0], ssg.at[1], rsg.at[1], after, x),
    ]

    step2 = []
    for h in range(2):
        for copy in step1[h * (ny - 1):(h + 1) * (ny - 1)]:
            copy.wait_recv()
        mine = y if h == 0 else z

        def add_axis(i, c, h=h, mine=mine):
            total = acc1[h, mine, i]
            for d in range(ny - 1):
                total = total + recv1[h, d, i].astype(f32)
            acc2[h, i] = total
            return c

        lax.fori_loop(0, nz, add_axis, 0)
        for d in range(nz - 1):
            to = z_peers[d] if h == 0 else y_peers[d]
            t = place(y, to, core) if h == 0 else place(to, z, core)
            step2.append(send(acc2.at[h, to], recv2.at[h, d], ss2.at[h, d], rs2.at[h, d], t, x))

    for copy in returns:
        copy.wait_recv()
    keep_u = mask_ref[...].astype(f32)
    for b in range(blocks):
        total = block_grad(FACE + b)
        if b < FACE:
            total = total + in_h[0, b].astype(f32)
        if b >= blocks - FACE:
            total = total + in_h[1, b - (blocks - FACE)].astype(f32)
        column = jnp.broadcast_to(keep_u[b:b + 1], total.shape).T
        grad_ref[b] = (column * total).astype(bf16)

    for h in range(2):
        for copy in step2[h * (nz - 1):(h + 1) * (nz - 1)]:
            copy.wait_recv()
        total = acc2[h, z if h == 0 else y]
        for d in range(nz - 1):
            total = total + recv2[h, d]
        share[h] = total
    recv3[x] = share[...]
    step3 = [
        send(share, recv3.at[x], ss3.at[d], rs3.at[d], tile, xx) for d, xx in enumerate(x_peers)
    ]
    for copy in step3:
        copy.wait_recv()
    total = recv3[0]
    for i in range(1, nx):
        total = total + recv3[i]
    total = total * scale
    half = HALF_T * TILE_ROWS
    sub_ref[0:half, :] = total[0]
    sub_ref[half:own, :] = total[1, 0:own - half]
    down_ref[:, 0:128] = total[1, TILE_ROWS:2 * TILE_ROWS]
    down_ref[:, 128:256] = total[1, 2 * TILE_ROWS:3 * TILE_ROWS]
    for copy in copies:
        copy.wait_send()


def on_device(
    features,
    w_sub,
    w_down,
    cotangent,
    vox_mask,
    nbr_owner,
    nbr_slot,
    voxel_map,
    parent_slot,
    parent_octant,
):
    _, blocks, voxels, channels = features.shape
    offsets = w_sub.shape[0]
    coarse_channels = w_down.shape[2]
    nx, tiles = lax.axis_size("dp"), lax.axis_size("tile")
    ny = 8
    nz = tiles // (2 * ny)
    f32, bf16, i32 = jnp.float32, jnp.bfloat16, jnp.int32
    tile_index = lax.axis_index("tile")
    owner, slot = nbr_owner[0], nbr_slot[0]
    present = owner >= 0
    position = jnp.where(present, (owner - tile_index) * blocks + FACE + slot, 0)
    octant = parent_octant[0]
    corner = (
        parent_slot[0] * voxels + 64 * (octant // 4) + 8 * ((octant // 2) % 2) + 2 * (octant % 2)
    )
    table = jnp.concatenate([
        position,
        jnp.where(present, 0, NO_VOXEL),
        jnp.pad(corner, (0, offsets - blocks))[None],
    ])
    entry = jnp.pad(
        position.T.reshape(1, -1), ((0, 0), (0, 256 - offsets * blocks)),
        constant_values=NO_BLOCK,
    )
    scale = float(nx * tiles * blocks * voxels) ** (-0.5)
    wide = blocks * voxels
    ext = blocks + 2 * FACE
    rows = HALF_T * TILE_ROWS
    own_rows = offsets * channels // tiles
    vmem = pl.BlockSpec(memory_space=pltpu.VMEM)
    smem = pl.BlockSpec(memory_space=pltpu.SMEM)
    dma = pltpu.SemaphoreType.DMA
    coarse_rows = cotangent.shape[1] * cotangent.shape[2]
    coarse, grad, sub, down = pl.pallas_call(
        functools.partial(kernel, (nx, ny, nz), scale),
        out_shape=(
            jax.ShapeDtypeStruct((coarse_rows, coarse_channels), bf16),
            jax.ShapeDtypeStruct((blocks, voxels, channels), bf16),
            jax.ShapeDtypeStruct((own_rows, channels), f32),
            jax.ShapeDtypeStruct((TILE_ROWS, coarse_channels), f32),
        ),
        in_specs=[smem] + [vmem] * 7,
        out_specs=(vmem,) * 4,
        scratch_shapes=[
            pltpu.VMEM((offsets, voxels, wide), bf16),
            pltpu.VMEM((offsets, channels, wide), bf16),
            pltpu.VMEM((ext, channels, voxels), bf16),
            pltpu.VMEM((2, FACE, channels, voxels), bf16),
            pltpu.VMEM((channels, offsets * channels), bf16),
            pltpu.VMEM((offsets, channels, channels), bf16),
            pltpu.VMEM((offsets * blocks, voxels, channels), bf16),
            pltpu.VMEM((blocks, PITCH, voxels), f32),
            pltpu.VMEM((channels, wide), f32),
            pltpu.VMEM((wide // 8, 8 * channels), bf16),
            pltpu.VMEM((wide, channels), f32),
            pltpu.VMEM((wide, channels), bf16),
            pltpu.VMEM((blocks // 2, 2 * voxels, 2 * channels), bf16),
            pltpu.VMEM((offsets * channels, channels), f32),
            pltpu.VMEM((8 * channels, coarse_channels), f32),
            pltpu.VMEM((TILE_ROWS, 256), i32),
            pltpu.SMEM((TILE_ROWS, 256), i32),
            pltpu.VMEM((offsets * blocks, voxels, channels), f32),
            pltpu.VMEM((2, 2, ny, nz, rows, 128), f32),
            pltpu.VMEM((2, ny, nz, rows, 128), bf16),
            pltpu.VMEM((2, ny, nz, rows, 128), bf16),
            pltpu.VMEM((2, ny, nz, rows, 128), f32),
            pltpu.VMEM((2, ny, nz, rows, 128), bf16),
            pltpu.VMEM((2, ny - 1, nz, rows, 128), bf16),
            pltpu.VMEM((2, nz, rows, 128), f32),
            pltpu.VMEM((2, nz - 1, rows, 128), f32),
            pltpu.VMEM((nx, 2, rows, 128), f32),
            pltpu.VMEM((2, rows, 128), f32),
            pltpu.VMEM((2, FACE, voxels, channels), bf16),
            pltpu.VMEM((2, FACE, voxels, channels), bf16),
            dma,
            dma((2,)), dma((2,)),
            dma((2, ny - 1)), dma((2, ny - 1)),
            dma((2, nz - 1)), dma((2, nz - 1)),
            dma((nx - 1,)), dma((nx - 1,)),
            dma((2,)), dma((2,)),
            dma((2,)), dma((2,)),
        ],
        compiler_params=pltpu.CompilerParams(
            collective_id=0, has_side_effects=True, vmem_limit_bytes=60 * 1024 * 1024
        ),
    )(
        table, entry, features[0], voxel_map[0], w_sub,
        w_down.reshape(-1, coarse_channels), cotangent[0].reshape(-1, coarse_channels),
        vox_mask[0],
    )
    return (
        coarse.reshape(cotangent.shape), grad[None], sub.reshape(-1), down.reshape(-1),
    )


def solution(mesh):
    in_specs = (
        P("dp", "tile", None, None),
        P(),
        P(),
        P("dp", "tile", None, None),
        P("dp", "tile", None),
        P("dp", "tile", None),
        P("dp", "tile", None),
        P("dp", "tile", None, None),
        P("dp", "tile"),
        P("dp", "tile"),
    )
    out_specs = (P("dp", "tile", None, None), P("dp", "tile", None, None), P("tile"), P("tile"))
    return jax.shard_map(
        on_device, mesh=mesh, in_specs=in_specs, out_specs=out_specs, check_vma=False
    )
```

time: 378 us -> 61.8 us (0.16)
  waiting for transfers between devices: 275 us -> 0 us
  matrix products: 57.4 us -> 0 us
  Pallas kernels: 0 us -> 52.6 us
  starting transfers between devices: 14.4 us -> 0 us
  between operations: 14.3 us -> 0.7 us
  other arithmetic: 8.1 us -> 0.63 us
    psum x1 -> x0, waiting for transfers between devices: 274 us -> none  [on_device(): total_sub, total_down = lax.psum((flat_sub, flat_down), ('tile', 'dp'))]
    dot_general x12 -> x0, matrix products: 57.4 us -> none  [the longest x1 18.4 us: return_terms(): jnp.einsum('bke,bkuc->euc', block_pick.astype(jnp.float32), terms, precis...]
    pallas_call x0 -> x1, Pallas kernels: none -> 52.6 us  [on_device(): pl.pallas_call(functools.partial(kernel, (nx, ny, nz), scale), out_shape=...]
    ppermute x4 -> x0, starting transfers between devices: 14.4 us -> none  [the longest x2 7.31 us: with_halo(): before = lax.ppermute(last, axis, up)]
    unnamed x8 -> x19, local copies, waits for them, and re-layouts: 2.61 us -> 6.58 us
  transfers between devices with their start and end apart: 5 -> 0, of which waited for: 2 -> 0; matrix products, arithmetic and copies ran while one was open for 3% -> 0% of each run, Pallas kernels for 0% -> 0%
where the time goes in v1:
time: 61.8 us; the launch traced here: 61.2 us
  Pallas kernels  52.6 us (85%)
  local copies, waits for them, and re-layouts  7.33 us (12%)
  between operations  0.7 us (1%)
  other arithmetic  0.63 us (1%)
    pallas_call x1, Pallas kernels, on_device(): pl.pallas_call(functools.partial(kernel, (nx, ny, nz), scale), out_shape=...  52.6 us
    unnamed x19, local copies, waits for them, and re-layouts  6.58 us

profile of v1, /device:TPU:1, one launch (start us, length us, event | category | flops | bytes accessed | tf_op | source)
XLA Modules:
  0.0 61.2 jit_solution(14292295774129091210)
XLA Ops:
  0.6 0.0 copy-start.5
  0.6 0.0 copy-start.6
  0.7 0.0 copy-start.4
  0.7 0.0 copy-start.3
  0.7 0.6 %copy-done.5 = s32[1,8]{1,0:T(1,128)S(1)} copy-done((s32[1,8]{1,0:T(1,128)S(1)}, s32[1,8]{1,0:T(1,128)}, u32[]{:S(2)}) %copy-start.5) | copy-done | bytes 56
  1.3 0.0 copy-done.6
  1.3 0.0 copy-done.4
  1.4 0.0 copy-done.3
  1.4 0.6 pad_add_fusion.table_ref
  2.0 0.1 copy.16
  2.1 0.1 reshape.34
  2.2 0.6 pad.9.erow_ref
  2.7 1.6 %copy.20 = s32[1,8,27,128]{3,2,1,0:T(8,128)} copy(s32[1,8,27,128]{3,1,2,0:T(8,128)} %param.17) | data formatting | bytes 221184 | tf_op args[7]
  4.3 52.6 %shard_map.129 = (bf16[512,256]{1,0:T(8,128)(2,1)}, bf16[8,128,128]{2,1,0:T(8,128)(2,1)}, f32[27,128]{1,0:T(8,128)}, f32[8,256]{1,0:T(8,128)}) custom-call(s32[17,27]{1,0:T(8,128)} %pad_add_fusion.table_ref, s32[1,256]{1,0:T(1,128)} %pad.9.erow_ref, bf16[8,128,128]{2,1,0:T(8,128)(2,1)} %bitcast.45, s32[8,27,128]{2,1,0:T(8,128)} %bitcast.42, ...), custom_call_target="tpu_custom_call" | custom-call | tf_op jit(solution)/shard_map/pallas_call | solution.py:386
  56.9 0.0 copy-start.2
  56.9 0.7 %copy-done.2 = f32[8,256]{1,0:T(8,128)S(1)} copy-done((f32[8,256]{1,0:T(8,128)S(1)}, f32[8,256]{1,0:T(8,128)}, u32[]{:S(2)}) %copy-start.2) | copy-done | bytes 8216
  57.6 0.6 copy.18
  58.2 0.0 copy-start
  58.2 1.7 %copy.24 = bf16[1,4,128,256]{3,2,1,0:T(8,128)(2,1)} copy(bf16[1,4,128,256]{3,2,1,0:T(8,128)(2,1)} %bitcast.44) | data formatting | bytes 524288
  59.9 0.0 copy-done
  59.9 0.0 copy-start.1
  59.9 0.7 %copy.25 = bf16[1,8,128,128]{3,2,1,0:T(8,128)(2,1)} copy(bf16[1,8,128,128]{3,2,1,0:T(8,128)(2,1)S(1)} %bitcast.43) | data formatting | bytes 524288
  60.6 0.0 copy-done.1
  60.6 0.6 copy.26
  (3 shorter events, 0.0 us)
Async XLA Ops:
  0.6 0.7 %copy-start.5 = (s32[1,8]{1,0:T(1,128)S(1)}, s32[1,8]{1,0:T(1,128)}, u32[]{:S(2)}) copy-start(s32[1,8]{1,0:T(1,128)} %param.19) | copy-start | bytes 100
  0.6 0.7 %copy-start.6 = (s32[1,8]{1,0:T(1,128)S(1)}, s32[1,8]{1,0:T(1,128)}, u32[]{:S(2)}) copy-start(s32[1,8]{1,0:T(1,128)} %param.18) | copy-start | bytes 100
  0.7 0.7 %copy-start.4 = (s32[1,8,27]{2,1,0:T(8,128)S(1)}, s32[1,8,27]{2,1,0:T(8,128)}, u32[]{:S(2)}) copy-start(s32[1,8,27]{2,1,0:T(8,128)} %param.15) | copy-start | bytes 2596
  0.7 0.7 %copy-start.3 = (s32[1,8,27]{2,1,0:T(8,128)S(1)}, s32[1,8,27]{2,1,0:T(8,128)}, u32[]{:S(2)}) copy-start(s32[1,8,27]{2,1,0:T(8,128)} %param.16) | copy-start | bytes 2596
  56.9 0.7 %copy-start.2 = (f32[8,256]{1,0:T(8,128)S(1)}, f32[8,256]{1,0:T(8,128)}, u32[]{:S(2)}) copy-start(f32[8,256]{1,0:T(8,128)} %get-tuple-element.11) | copy-start | bytes 24580
  58.2 1.7 %copy-start = (bf16[8,128,128]{2,1,0:T(8,128)(2,1)S(1)}, bf16[8,128,128]{2,1,0:T(8,128)(2,1)}, u32[]{:S(2)}) copy-start(bf16[8,128,128]{2,1,0:T(8,128)(2,1)} %get-tuple-element.9) | copy-start | bytes 786436
  59.9 0.7 %copy-start.1 = (f32[27,128]{1,0:T(8,128)S(1)}, f32[27,128]{1,0:T(8,128)}, u32[]{:S(2)}) copy-start(f32[27,128]{1,0:T(8,128)} %get-tuple-element.10) | copy-start | bytes 41476

commit v2 on v1

--- a/solution.py
+++ b/solution.py
@@ -11,7 +11,6 @@
 MESH = pl.DeviceIdType.MESH
 TILE_ROWS = 8
 HALF_T = 3
-PITCH = 32
 NO_BLOCK = 99
 NO_VOXEL = 1000
 
@@ -118,8 +117,7 @@
     perm = (
         lax.broadcasted_iota(jnp.int32, (voxels, voxels), 0) == child_order((voxels, voxels))
     ).astype(bf16)
-    for b in range(blocks):
-        map_p[b, 0:offsets, :] = dot(map_ref[b].astype(bf16), perm)
+    map_p[...] = dot(map_ref[...].astype(bf16), perm)
     keep = dot(masks, perm)
     row_ids = lax.broadcasted_iota(jnp.int32, (voxels, voxels), 0).astype(f32)
 
@@ -133,8 +131,9 @@
         def body(k, c):
             if weights:
                 transpose_weight(k, c)
+            maps = map_p[pl.ds(pl.multiple_of(k * blocks, blocks), blocks), :]
             for b in some:
-                row = map_p[b, pl.ds(k, 1), :] - table_ref[blocks + b, k].astype(f32)
+                row = maps[b:b + 1] - table_ref[blocks + b, k].astype(f32)
                 tile_bk = (row_ids == row).astype(bf16)
                 picks[k, :, lanes(b)] = tile_bk
                 gathered[k, :, lanes(b)] = dot(ext_t[table_ref[b, k]], tile_bk).astype(bf16)
@@ -195,18 +194,28 @@
     chip_rows = offsets * channels // (ny * nz)
     own = chip_rows // 2
 
-    def stage(yy, c):
+    full = HALF_T * TILE_ROWS
+
+    def stage_first(yy, c):
+        first = pl.multiple_of(yy * nz * chip_rows, 16)
+        slab = grad_sub[pl.ds(first, nz * chip_rows), :]
+        for zz in range(nz):
+            for cc in range(2):
+                start = (zz * 2 + cc) * own
+                parts[cc, 0, yy, zz] = slab[start:start + full]
+        send0[0, yy] = parts[other, 0, yy].astype(bf16)
+        return c
+
+    def stage_second(yy, c):
         first = pl.multiple_of(yy * nz * chip_rows, 16)
         slab = grad_sub[pl.ds(first, nz * chip_rows), :]
         down = grad_down[pl.ds(pl.multiple_of(yy * channels, channels), channels), :]
         for zz in range(nz):
             for cc in range(2):
                 start = (zz * 2 + cc) * own
-                parts[cc, 0, yy, zz] = slab[start:start + HALF_T * TILE_ROWS]
-                rest = own - HALF_T * TILE_ROWS
-                last = slab[start + HALF_T * TILE_ROWS:start + own]
                 parts[cc, 1, zz, yy, 0:TILE_ROWS, :] = jnp.concatenate(
-                    [last, jnp.zeros((TILE_ROWS - rest, channels), f32)], axis=0
+                    [slab[start + full:start + own], jnp.zeros((TILE_ROWS - own + full, channels), f32)],
+                    axis=0,
                 )
                 start = (zz * 2 + cc) * TILE_ROWS
                 for i in range(2):
@@ -216,17 +225,18 @@
                     ]
         return c
 
-    lax.fori_loop(0, ny, stage, 0)
-
-    step0 = []
-    for h in range(2):
-        def cast_half(i, c, h=h):
-            send0[h, i] = parts[other, h, i].astype(bf16)
-            return c
-        lax.fori_loop(0, ny, cast_half, 0)
-        step0.append(
-            send(send0.at[h], recv0.at[h], ss0.at[h], rs0.at[h], place(y, z, other), x)
-        )
+    def cast_second(i, c):
+        send0[1, i] = parts[other, 1, i].astype(bf16)
+        return c
+
+    def send_half(h):
+        return send(send0.at[h], recv0.at[h], ss0.at[h], rs0.at[h], place(y, z, other), x)
+
+    lax.fori_loop(0, ny, stage_first, 0)
+    step0 = [send_half(0)]
+    lax.fori_loop(0, ny, stage_second, 0)
+    lax.fori_loop(0, nz, cast_second, 0)
+    step0.append(send_half(1))
 
     def spread(j, c):
         rows = pl.ds(pl.multiple_of(j * 3 * voxels, voxels), 3 * voxels)
@@ -240,7 +250,8 @@
                     ]
         return c
 
-    lax.fori_loop(0, offsets // 3, spread, 0)
+    early = offsets // 9
+    lax.fori_loop(0, early, spread, 0)
 
     step1 = []
     for h in range(2):
@@ -258,6 +269,7 @@
             t = place(to, z, core) if h == 0 else place(y, to, core)
             step1.append(send(send1.at[h, to], recv1.at[h, d], ss1.at[h, d], rs1.at[h, d], t, x))
 
+    lax.fori_loop(early, offsets // 3, spread, 0)
     sort_copy.wait()
 
     def term(i, running):
@@ -332,10 +344,26 @@
     half = HALF_T * TILE_ROWS
     sub_ref[0:half, :] = total[0]
     sub_ref[half:own, :] = total[1, 0:own - half]
-    down_ref[:, 0:128] = total[1, TILE_ROWS:2 * TILE_ROWS]
-    down_ref[:, 128:256] = total[1, 2 * TILE_ROWS:3 * TILE_ROWS]
+    for i in range(2):
+        down_ref[pl.ds(i, TILE_ROWS, 2), :] = total[1, (i + 1) * TILE_ROWS:(i + 2) * TILE_ROWS]
     for copy in copies:
         copy.wait_send()
+
+
+def finish_kernel(*refs):
+    arrays = len(refs) // 2
+    for source, result in zip(refs[:arrays], refs[arrays:]):
+        result[...] = source[...]
+
+
+def finish(*arrays):
+    vmem = pl.BlockSpec(memory_space=pltpu.VMEM)
+    return pl.pallas_call(
+        finish_kernel,
+        out_shape=tuple(jax.ShapeDtypeStruct(a.shape, a.dtype) for a in arrays),
+        in_specs=[vmem] * len(arrays),
+        out_specs=(vmem,) * len(arrays),
+    )(*arrays)
 
 
 def on_device(
@@ -370,6 +398,7 @@
         jnp.where(present, 0, NO_VOXEL),
         jnp.pad(corner, (0, offsets - blocks))[None],
     ])
+    maps = jnp.transpose(voxel_map[0], (1, 0, 2)).reshape(-1, voxels)
     entry = jnp.pad(
         position.T.reshape(1, -1), ((0, 0), (0, 256 - offsets * blocks)),
         constant_values=NO_BLOCK,
@@ -389,7 +418,7 @@
             jax.ShapeDtypeStruct((coarse_rows, coarse_channels), bf16),
             jax.ShapeDtypeStruct((blocks, voxels, channels), bf16),
             jax.ShapeDtypeStruct((own_rows, channels), f32),
-            jax.ShapeDtypeStruct((TILE_ROWS, coarse_channels), f32),
+            jax.ShapeDtypeStruct((2 * TILE_ROWS, channels), f32),
         ),
         in_specs=[smem] + [vmem] * 7,
         out_specs=(vmem,) * 4,
@@ -401,7 +430,7 @@
             pltpu.VMEM((channels, offsets * channels), bf16),
             pltpu.VMEM((offsets, channels, channels), bf16),
             pltpu.VMEM((offsets * blocks, voxels, channels), bf16),
-            pltpu.VMEM((blocks, PITCH, voxels), f32),
+            pltpu.VMEM((offsets * blocks, voxels), f32),
             pltpu.VMEM((channels, wide), f32),
             pltpu.VMEM((wide // 8, 8 * channels), bf16),
             pltpu.VMEM((wide, channels), f32),
@@ -436,10 +465,11 @@
             collective_id=0, has_side_effects=True, vmem_limit_bytes=60 * 1024 * 1024
         ),
     )(
-        table, entry, features[0], voxel_map[0], w_sub,
+        table, entry, features[0], maps, w_sub,
         w_down.reshape(-1, coarse_channels), cotangent[0].reshape(-1, coarse_channels),
         vox_mask[0],
     )
+    coarse, grad, sub, down = finish(coarse, grad, sub, down)
     return (
         coarse.reshape(cotangent.shape), grad[None], sub.reshape(-1), down.reshape(-1),
     )

time: 61.8 us -> 57.1 us (0.924)
  local copies, waits for them, and re-layouts: 7.33 us -> 1.42 us
  Pallas kernels: 52.6 us -> 54.1 us
    unnamed x19 -> x8, local copies, waits for them, and re-layouts: 6.58 us -> 0.67 us
    pallas_call x0 -> x1, Pallas kernels: none -> 1.85 us  [finish(): pl.pallas_call(finish_kernel, out_shape=tuple((jax.ShapeDtypeStruct(a.sha...]
where the time goes in v2:
time: 57.1 us; the launch traced here: 56.9 us
  Pallas kernels  54.1 us (95%)
  local copies, waits for them, and re-layouts  1.42 us (2%)
  between operations  0.69 us (1%)
  other arithmetic  0.63 us (1%)
    pallas_call x1, Pallas kernels, on_device(): pl.pallas_call(functools.partial(kernel, (nx, ny, nz), scale), out_shape=...  52.3 us
    pallas_call x1, Pallas kernels, finish(): pl.pallas_call(finish_kernel, out_shape=tuple((jax.ShapeDtypeStruct(a.sha...  1.85 us

profile of v2, /device:TPU:1, one launch (start us, length us, event | category | flops | bytes accessed | tf_op | source)
XLA Modules:
  0.0 56.9 jit_solution(7944479133571948245)
XLA Ops:
  0.6 0.0 copy-start.2
  0.6 0.0 copy-start.3
  0.7 0.0 copy-start.1
  0.7 0.0 copy-start
  0.7 0.6 %copy-done.2 = s32[1,8]{1,0:T(1,128)S(1)} copy-done((s32[1,8]{1,0:T(1,128)S(1)}, s32[1,8]{1,0:T(1,128)}, u32[]{:S(2)}) %copy-start.2) | copy-done | bytes 56
  1.3 0.0 copy-done.3
  1.3 0.0 copy-done.1
  1.4 0.0 copy-done
  1.4 0.6 %pad_add_fusion.table_ref = s32[17,27]{1,0:T(8,128)} fusion(s32[1,27]{1,0:T(1,128)S(1)} %pad_bitcast_fusion, s32[8,27]{1,0:T(8,128)S(1)} %get-tuple-element.22, s32[8,27]{1,0:T(8,128)S(1)} %get-tuple-element.21), kind=kLoop, calls=%fused_computation | loop fusion | flops 918 | bytes 3672 | tf_op jit(solution)/shard_map/concatenate | solution.py:396
  2.0 0.1 copy.15
  2.1 0.1 reshape.37
  2.2 0.6 %pad.9.erow_ref = s32[1,256]{1,0:T(1,128)} pad(s32[1,216]{1,0:T(1,128)S(1)} %reshape.37, s32[]{:T(128)} %constant.61.clone.1), padding=0_0x0_40 | pad | bytes 1892 | tf_op jit(solution)/shard_map/jit(_pad)/pad | solution.py:402
  2.7 52.3 %shard_map.129 = (bf16[512,256]{1,0:T(8,128)(2,1)}, bf16[8,128,128]{2,1,0:T(8,128)(2,1)}, f32[27,128]{1,0:T(8,128)}, f32[16,128]{1,0:T(8,128)}) custom-call(s32[17,27]{1,0:T(8,128)} %pad_add_fusion.table_ref, s32[1,256]{1,0:T(1,128)} %pad.9.erow_ref, bf16[8,128,128]{2,1,0:T(8,128)(2,1)} %bitcast.43, s32[216,128]{1,0:T(8,128)} %bitcast.45, ...), custom_call_target="tpu_custom_call" | custom-call | tf_op jit(solution)/shard_map/pallas_call | solution.py:415
  55.0 1.8 %shard_map.130 = (bf16[512,256]{1,0:T(8,128)(2,1)}, bf16[8,128,128]{2,1,0:T(8,128)(2,1)}, f32[27,128]{1,0:T(8,128)}, f32[16,128]{1,0:T(8,128)}) custom-call(bf16[512,256]{1,0:T(8,128)(2,1)} %get-tuple-element.12.refs_0_, bf16[8,128,128]{2,1,0:T(8,128)(2,1)} %get-tuple-element.13.refs_1_, f32[27,128]{1,0:T(8,128)} %get-tuple-element.14.refs_2_, ...), custom_call_target="tpu_custom_call" | custom-call | tf_op jit(solution)/shard_map/pallas_call | solution.py:361
  (3 shorter events, 0.0 us)
Async XLA Ops:
  0.6 0.7 %copy-start.2 = (s32[1,8]{1,0:T(1,128)S(1)}, s32[1,8]{1,0:T(1,128)}, u32[]{:S(2)}) copy-start(s32[1,8]{1,0:T(1,128)} %param.19) | copy-start | bytes 100
  0.6 0.7 %copy-start.3 = (s32[1,8]{1,0:T(1,128)S(1)}, s32[1,8]{1,0:T(1,128)}, u32[]{:S(2)}) copy-start(s32[1,8]{1,0:T(1,128)} %param.18) | copy-start | bytes 100
  0.7 0.7 %copy-start.1 = (s32[1,8,27]{2,1,0:T(8,128)S(1)}, s32[1,8,27]{2,1,0:T(8,128)}, u32[]{:S(2)}) copy-start(s32[1,8,27]{2,1,0:T(8,128)} %param.15) | copy-start | bytes 2596
  0.7 0.7 %copy-start = (s32[1,8,27]{2,1,0:T(8,128)S(1)}, s32[1,8,27]{2,1,0:T(8,128)}, u32[]{:S(2)}) copy-start(s32[1,8,27]{2,1,0:T(8,128)} %param.16) | copy-start | bytes 2596

commit v3 on v2

--- a/solution.py
+++ b/solution.py
@@ -138,7 +138,7 @@
                 picks[k, :, lanes(b)] = tile_bk
                 gathered[k, :, lanes(b)] = dot(ext_t[table_ref[b, k]], tile_bk).astype(bf16)
             return c
-        lax.fori_loop(0, offsets, body, 0, unroll=3)
+        lax.fori_loop(0, offsets, body, 0, unroll=9)
 
     gather(range(FACE, blocks - FACE), True)
     for copy in halo:
@@ -189,7 +189,7 @@
         grad_sub[rows, :] = dot(flat_g[rows, :], dpre[...])
         return c
 
-    lax.fori_loop(0, offsets // 3, weight_grad, 0)
+    lax.fori_loop(0, offsets // 3, weight_grad, 0, unroll=3)
 
     chip_rows = offsets * channels // (ny * nz)
     own = chip_rows // 2
@@ -279,7 +279,7 @@
         return running
 
     lax.fori_loop(
-        0, offsets * blocks, term, jnp.zeros((voxels, channels), f32), unroll=4
+        0, offsets * blocks, term, jnp.zeros((voxels, channels), f32), unroll=8
     )
 
     def block_grad(e):

time: 57.1 us -> 54.7 us (0.958)
  Pallas kernels: 54.1 us -> 51.8 us
    pallas_call x1, Pallas kernels: 52.3 us -> 49.9 us  [on_device(): pl.pallas_call(functools.partial(kernel, (nx, ny, nz), scale), out_shape=...]
where the time goes in v3:
time: 54.7 us; the launch traced here: 54.5 us
  Pallas kernels  51.8 us (95%)
  local copies, waits for them, and re-layouts  1.42 us (3%)
  between operations  0.69 us (1%)
  other arithmetic  0.63 us (1%)
    pallas_call x1, Pallas kernels, on_device(): pl.pallas_call(functools.partial(kernel, (nx, ny, nz), scale), out_shape=...  49.9 us
    pallas_call x1, Pallas kernels, finish(): pl.pallas_call(finish_kernel, out_shape=tuple((jax.ShapeDtypeStruct(a.sha...  1.85 us

profile of v3, /device:TPU:1, one launch (start us, length us, event | category | flops | bytes accessed | tf_op | source)
XLA Modules:
  0.0 54.5 jit_solution(17271752137128396286)
XLA Ops:
  0.6 0.0 copy-start.2
  0.6 0.0 copy-start.3
  0.7 0.0 copy-start.1
  0.7 0.0 copy-start
  0.7 0.6 %copy-done.2 = s32[1,8]{1,0:T(1,128)S(1)} copy-done((s32[1,8]{1,0:T(1,128)S(1)}, s32[1,8]{1,0:T(1,128)}, u32[]{:S(2)}) %copy-start.2) | copy-done | bytes 56
  1.3 0.0 copy-done.3
  1.3 0.0 copy-done.1
  1.4 0.0 copy-done
  1.4 0.6 %pad_add_fusion.table_ref = s32[17,27]{1,0:T(8,128)} fusion(s32[1,27]{1,0:T(1,128)S(1)} %pad_bitcast_fusion, s32[8,27]{1,0:T(8,128)S(1)} %get-tuple-element.22, s32[8,27]{1,0:T(8,128)S(1)} %get-tuple-element.21), kind=kLoop, calls=%fused_computation | loop fusion | flops 918 | bytes 3672 | tf_op jit(solution)/shard_map/concatenate | solution.py:396
  2.0 0.1 copy.15
  2.1 0.1 reshape.37
  2.2 0.6 %pad.9.erow_ref = s32[1,256]{1,0:T(1,128)} pad(s32[1,216]{1,0:T(1,128)S(1)} %reshape.37, s32[]{:T(128)} %constant.61.clone.1), padding=0_0x0_40 | pad | bytes 1892 | tf_op jit(solution)/shard_map/jit(_pad)/pad | solution.py:402
  2.7 49.9 %shard_map.129 = (bf16[512,256]{1,0:T(8,128)(2,1)}, bf16[8,128,128]{2,1,0:T(8,128)(2,1)}, f32[27,128]{1,0:T(8,128)}, f32[16,128]{1,0:T(8,128)}) custom-call(s32[17,27]{1,0:T(8,128)} %pad_add_fusion.table_ref, s32[1,256]{1,0:T(1,128)} %pad.9.erow_ref, bf16[8,128,128]{2,1,0:T(8,128)(2,1)} %bitcast.43, s32[216,128]{1,0:T(8,128)} %bitcast.45, ...), custom_call_target="tpu_custom_call" | custom-call | tf_op jit(solution)/shard_map/pallas_call | solution.py:415
  52.7 1.8 %shard_map.130 = (bf16[512,256]{1,0:T(8,128)(2,1)}, bf16[8,128,128]{2,1,0:T(8,128)(2,1)}, f32[27,128]{1,0:T(8,128)}, f32[16,128]{1,0:T(8,128)}) custom-call(bf16[512,256]{1,0:T(8,128)(2,1)} %get-tuple-element.12.refs_0_, bf16[8,128,128]{2,1,0:T(8,128)(2,1)} %get-tuple-element.13.refs_1_, f32[27,128]{1,0:T(8,128)} %get-tuple-element.14.refs_2_, ...), custom_call_target="tpu_custom_call" | custom-call | tf_op jit(solution)/shard_map/pallas_call | solution.py:361
  (3 shorter events, 0.0 us)
Async XLA Ops:
  0.6 0.7 %copy-start.2 = (s32[1,8]{1,0:T(1,128)S(1)}, s32[1,8]{1,0:T(1,128)}, u32[]{:S(2)}) copy-start(s32[1,8]{1,0:T(1,128)} %param.19) | copy-start | bytes 100
  0.6 0.7 %copy-start.3 = (s32[1,8]{1,0:T(1,128)S(1)}, s32[1,8]{1,0:T(1,128)}, u32[]{:S(2)}) copy-start(s32[1,8]{1,0:T(1,128)} %param.18) | copy-start | bytes 100
  0.7 0.7 %copy-start.1 = (s32[1,8,27]{2,1,0:T(8,128)S(1)}, s32[1,8,27]{2,1,0:T(8,128)}, u32[]{:S(2)}) copy-start(s32[1,8,27]{2,1,0:T(8,128)} %param.15) | copy-start | bytes 2596
  0.7 0.7 %copy-start = (s32[1,8,27]{2,1,0:T(8,128)S(1)}, s32[1,8,27]{2,1,0:T(8,128)}, u32[]{:S(2)}) copy-start(s32[1,8,27]{2,1,0:T(8,128)} %param.16) | copy-start | bytes 2596

commit v4 on v3

--- a/solution.py
+++ b/solution.py
@@ -108,11 +108,6 @@
         send(ext_t.at[pl.ds(FACE, FACE)], halo_in.at[1], ssh.at[0], rsh.at[0], before, x),
         send(ext_t.at[pl.ds(blocks, FACE)], halo_in.at[0], ssh.at[1], rsh.at[1], after, x),
     ]
-    sort_v[...] = jnp.zeros_like(sort_v)
-    for i, row in enumerate(sort_rows(erow_ref[...], offsets * blocks)):
-        sort_v[i:i + 1, :] = row
-    sort_copy = pltpu.make_async_copy(sort_v, sort_s, sort_sem)
-    sort_copy.start()
 
     perm = (
         lax.broadcasted_iota(jnp.int32, (voxels, voxels), 0) == child_order((voxels, voxels))
@@ -170,8 +165,6 @@
     scatter = (
         lax.broadcasted_iota(jnp.int32, (cot_ref.shape[0], voxels), 0) == target
     ).astype(bf16)
-    partial_value = dot(hidden[...], wd_ref[...]).astype(bf16)
-    coarse_ref[...] = dot(scatter, partial_value).astype(bf16)
     picked = dot(scatter, cot_ref[...], ((0,), (0,))).astype(bf16)
     dchildren = dot(picked, wd_ref[...], ((1,), (1,)))
     grad_down[...] = dot(hidden[...], picked, ((0,), (0,)))
@@ -269,6 +262,13 @@
             t = place(to, z, core) if h == 0 else place(y, to, core)
             step1.append(send(send1.at[h, to], recv1.at[h, d], ss1.at[h, d], rs1.at[h, d], t, x))
 
+    sort_v[...] = jnp.zeros_like(sort_v)
+    for i, row in enumerate(sort_rows(erow_ref[...], offsets * blocks)):
+        sort_v[i:i + 1, :] = row
+    sort_copy = pltpu.make_async_copy(sort_v, sort_s, sort_sem)
+    sort_copy.start()
+    partial_value = dot(hidden[...], wd_ref[...]).astype(bf16)
+    coarse_ref[...] = dot(scatter, partial_value).astype(bf16)
     lax.fori_loop(early, offsets // 3, spread, 0)
     sort_copy.wait()
 

time: 54.7 us -> 54.3 us (level)
  no operation moved by 1% of the time
where the time goes in v4:
time: 54.3 us; the launch traced here: 54.1 us
  Pallas kernels  51.4 us (95%)
  local copies, waits for them, and re-layouts  1.42 us (3%)
  between operations  0.69 us (1%)
  other arithmetic  0.63 us (1%)
    pallas_call x1, Pallas kernels, on_device(): pl.pallas_call(functools.partial(kernel, (nx, ny, nz), scale), out_shape=...  49.5 us
    pallas_call x1, Pallas kernels, finish(): pl.pallas_call(finish_kernel, out_shape=tuple((jax.ShapeDtypeStruct(a.sha...  1.85 us

profile of v4, /device:TPU:1, one launch (start us, length us, event | category | flops | bytes accessed | tf_op | source)
XLA Modules:
  0.0 54.1 jit_solution(6609560479165322268)
XLA Ops:
  0.6 0.0 copy-start.2
  0.6 0.0 copy-start.3
  0.7 0.0 copy-start.1
  0.7 0.0 copy-start
  0.7 0.6 %copy-done.2 = s32[1,8]{1,0:T(1,128)S(1)} copy-done((s32[1,8]{1,0:T(1,128)S(1)}, s32[1,8]{1,0:T(1,128)}, u32[]{:S(2)}) %copy-start.2) | copy-done | bytes 56
  1.3 0.0 copy-done.3
  1.3 0.0 copy-done.1
  1.4 0.0 copy-done
  1.4 0.6 %pad_add_fusion.table_ref = s32[17,27]{1,0:T(8,128)} fusion(s32[1,27]{1,0:T(1,128)S(1)} %pad_bitcast_fusion, s32[8,27]{1,0:T(8,128)S(1)} %get-tuple-element.22, s32[8,27]{1,0:T(8,128)S(1)} %get-tuple-element.21), kind=kLoop, calls=%fused_computation | loop fusion | flops 918 | bytes 3672 | tf_op jit(solution)/shard_map/concatenate | solution.py:396
  2.0 0.1 copy.15
  2.1 0.1 reshape.37
  2.2 0.6 %pad.9.erow_ref = s32[1,256]{1,0:T(1,128)} pad(s32[1,216]{1,0:T(1,128)S(1)} %reshape.37, s32[]{:T(128)} %constant.61.clone.1), padding=0_0x0_40 | pad | bytes 1892 | tf_op jit(solution)/shard_map/jit(_pad)/pad | solution.py:402
  2.7 49.5 %shard_map.129 = (bf16[512,256]{1,0:T(8,128)(2,1)}, bf16[8,128,128]{2,1,0:T(8,128)(2,1)}, f32[27,128]{1,0:T(8,128)}, f32[16,128]{1,0:T(8,128)}) custom-call(s32[17,27]{1,0:T(8,128)} %pad_add_fusion.table_ref, s32[1,256]{1,0:T(1,128)} %pad.9.erow_ref, bf16[8,128,128]{2,1,0:T(8,128)(2,1)} %bitcast.43, s32[216,128]{1,0:T(8,128)} %bitcast.45, ...), custom_call_target="tpu_custom_call" | custom-call | tf_op jit(solution)/shard_map/pallas_call | solution.py:415
  52.3 1.8 %shard_map.130 = (bf16[512,256]{1,0:T(8,128)(2,1)}, bf16[8,128,128]{2,1,0:T(8,128)(2,1)}, f32[27,128]{1,0:T(8,128)}, f32[16,128]{1,0:T(8,128)}) custom-call(bf16[512,256]{1,0:T(8,128)(2,1)} %get-tuple-element.12.refs_0_, bf16[8,128,128]{2,1,0:T(8,128)(2,1)} %get-tuple-element.13.refs_1_, f32[27,128]{1,0:T(8,128)} %get-tuple-element.14.refs_2_, ...), custom_call_target="tpu_custom_call" | custom-call | tf_op jit(solution)/shard_map/pallas_call | solution.py:361
  (3 shorter events, 0.0 us)
Async XLA Ops:
  0.6 0.7 %copy-start.2 = (s32[1,8]{1,0:T(1,128)S(1)}, s32[1,8]{1,0:T(1,128)}, u32[]{:S(2)}) copy-start(s32[1,8]{1,0:T(1,128)} %param.19) | copy-start | bytes 100
  0.6 0.7 %copy-start.3 = (s32[1,8]{1,0:T(1,128)S(1)}, s32[1,8]{1,0:T(1,128)}, u32[]{:S(2)}) copy-start(s32[1,8]{1,0:T(1,128)} %param.18) | copy-start | bytes 100
  0.7 0.7 %copy-start.1 = (s32[1,8,27]{2,1,0:T(8,128)S(1)}, s32[1,8,27]{2,1,0:T(8,128)}, u32[]{:S(2)}) copy-start(s32[1,8,27]{2,1,0:T(8,128)} %param.15) | copy-start | bytes 2596
  0.7 0.7 %copy-start = (s32[1,8,27]{2,1,0:T(8,128)S(1)}, s32[1,8,27]{2,1,0:T(8,128)}, u32[]{:S(2)}) copy-start(s32[1,8,27]{2,1,0:T(8,128)} %param.16) | copy-start | bytes 2596
